TPU v7x, 32 devices: a whole 2x2x4 slice. The times are simulated.
32 devices in a mesh: ens: 2 (over x), fn: 16 (over z, y, core).
Axes of the slice: x: 2, y: 2, z: 4, core: 2. Of those that a mesh axis runs over, the one named last changes fastest.
Arguments:
- sensor_values: bfloat16 [8192, 1024], P(('ens', 'fn')), parts along dimension 0, may hold values from -6 to 6
- amplitude: float32 [8192], P(('ens', 'fn')), parts along dimension 0, may hold values from 0.3 to 1.5
- field_modes: int32 [8192, 2], P(('ens', 'fn')), parts along dimension 0, may hold values from 1 to 5
- point_index: int32 [256, 2], P(('ens', 'fn')), parts along dimension 0, may hold values from 0 to 127
- forcing: bfloat16 [256], P(('ens', 'fn')), parts along dimension 0, may hold values from -6 to 6
- branch_in: bfloat16 [1024, 512], replicated, may hold values from -0.1875 to 0.1875
- branch_in_bias: float32 [512], replicated, may hold values from -3 to 3
- branch_out: bfloat16 [512, 512], replicated, may hold values from -0.046875 to 0.046875
- branch_out_bias: float32 [512], replicated, may hold values from -0.6 to 0.6
- trunk_in: float32 [2, 512], replicated, may hold values from -8 to 8
- trunk_in_bias: float32 [512], replicated, may hold values from -4 to 4
- trunk_out: bfloat16 [512, 512], replicated, may hold values from -0.25 to 0.25
- trunk_out_bias: float32 [512], replicated, may hold values from -3 to 3
Outputs:
- grad_branch_in: float32 [2048, 512], P(('ens', 'fn')), parts along dimension 0
- grad_branch_out: float32 [1024, 512], P(('ens', 'fn')), parts along dimension 0
- grad_trunk_out: float32 [1024, 512], P(('ens', 'fn')), parts along dimension 0
There are 2 independent parts, one for each index of `ens`. A program takes and returns all parts, laid end to end along the dimension named above; an argument that names none is the same for every part. Nothing has to cross between parts.
All inputs are finite; a program needn't handle non-finite values.
Results may differ from a plain program's by a relative error of at most 0.0057.
Values may be sent and summed in bfloat16 or wider, within the bound.
A program may use at most 64 MiB of HBM per device.

v0:
```python
import math

import jax
import jax.numpy as jnp
from jax import lax
from jax.sharding import PartitionSpec as P

GRID = 128


def grid_coords(point_index):
    return (point_index.astype(jnp.float32) + 0.5) / GRID


def trunk_hidden(coords, trunk_in, trunk_in_bias):
    pre_act = (
        coords[:, 0:1] * trunk_in[0][None, :]
        + coords[:, 1:2] * trunk_in[1][None, :]
        + trunk_in_bias[None, :]
    )
    activ = jnp.tanh(pre_act)
    first_der = 1.0 - activ * activ
    second_der = -2.0 * activ * first_der
    square_sum = trunk_in[0] * trunk_in[0] + trunk_in[1] * trunk_in[1]
    stacked = jnp.stack(
        [activ, first_der * trunk_in[0], first_der * trunk_in[1], second_der * square_sum], axis=1
    )
    return stacked.astype(jnp.bfloat16)


def trunk_tangents(hidden, trunk_out, trunk_out_bias):
    npts = hidden.shape[0]
    width = trunk_out.shape[1]
    flat_out = jnp.dot(
        hidden.reshape(npts * 4, hidden.shape[2]), trunk_out, preferred_element_type=jnp.float32
    )
    chan_mask = (jnp.arange(4) == 0).astype(jnp.float32)
    shaped = (
        flat_out.reshape(npts, 4, width) + chan_mask[None, :, None] * trunk_out_bias[None, None, :]
    )
    return shaped.astype(jnp.bfloat16)


def tile_cotangent(branch_feat, tangents, coords, forcing_pts, amplitude, field_modes):
    npts = tangents.shape[0]
    nfield = branch_feat.shape[0]
    flattened = tangents.reshape(npts * 4, tangents.shape[2])
    tile_vals = lax.dot_general(
        branch_feat, flattened, (((1,), (1,)), ((), ())), preferred_element_type=jnp.float32
    )
    tile_vals = tile_vals.reshape(nfield, npts, 4)
    x_coord = coords[:, 0][None, :]
    y_coord = coords[:, 1][None, :]
    freq_x = field_modes[:, 0:1].astype(jnp.float32) * math.pi
    freq_y = field_modes[:, 1:2].astype(jnp.float32) * math.pi
    amp_col = amplitude[:, None]
    sin_x = jnp.sin(freq_x * x_coord)
    cos_x = jnp.cos(freq_x * x_coord)
    sin_y = jnp.sin(freq_y * y_coord)
    cos_y = jnp.cos(freq_y * y_coord)
    perm = jnp.exp(amp_col * sin_x * sin_y)
    perm_dx = perm * amp_col * freq_x * cos_x * sin_y
    perm_dy = perm * amp_col * freq_y * sin_x * cos_y
    residual_tile = (
        tile_vals[:, :, 0]
        - (perm * tile_vals[:, :, 3] + perm_dx * tile_vals[:, :, 1] + perm_dy * tile_vals[:, :, 2])
        - forcing_pts.astype(jnp.float32)[None, :]
    )
    scaled = residual_tile / npts
    stacked = jnp.stack([scaled, -scaled * perm_dx, -scaled * perm_dy, -scaled * perm], axis=2)
    return stacked.astype(jnp.bfloat16).reshape(nfield, npts * 4)


def trunk_weight_grad(hidden_rows, d_tangents):
    upper_part = lax.optimization_barrier(d_tangents.astype(jnp.bfloat16))
    lower_part = (d_tangents - upper_part.astype(jnp.float32)).astype(jnp.bfloat16)
    dims = (((0,), (0,)), ((), ()))
    upper_term = lax.dot_general(hidden_rows, upper_part, dims, preferred_element_type=jnp.float32)
    lower_term = lax.dot_general(hidden_rows, lower_part, dims, preferred_element_type=jnp.float32)
    return upper_term + lower_term


def per_device(
    sensor_values,
    amplitude,
    field_modes,
    point_index,
    forcing,
    branch_in,
    branch_in_bias,
    branch_out,
    branch_out_bias,
    trunk_in,
    trunk_in_bias,
    trunk_out,
    trunk_out_bias,
):
    width = trunk_out.shape[1]
    trunk_width = trunk_out.shape[0]
    branch_hidden = jnp.tanh(
        jnp.dot(sensor_values, branch_in, preferred_element_type=jnp.float32)
        + branch_in_bias[None, :]
    ).astype(jnp.bfloat16)
    branch_feat = (
        jnp.dot(branch_hidden, branch_out, preferred_element_type=jnp.float32)
        + branch_out_bias[None, :]
    ).astype(jnp.bfloat16)
    own_coords = grid_coords(point_index)
    hidden_own = trunk_hidden(own_coords, trunk_in, trunk_in_bias)
    tangents_own = trunk_tangents(hidden_own, trunk_out, trunk_out_bias)
    tangents_all, coords_sent, forcing_all = (
        lax.all_gather(tangents_own, "fn", axis=0, tiled=True),
        lax.all_gather(own_coords.astype(jnp.bfloat16), "fn", axis=0, tiled=True),
        lax.all_gather(forcing, "fn", axis=0, tiled=True),
    )
    coords_all = coords_sent.astype(jnp.float32)
    all_points = tangents_all.shape[0]
    cotangent = tile_cotangent(
        branch_feat, tangents_all, coords_all, forcing_all, amplitude, field_modes
    )
    flattened = tangents_all.reshape(all_points * 4, width)
    d_branch = jnp.dot(cotangent, flattened, preferred_element_type=jnp.float32).astype(
        jnp.bfloat16
    )
    grad_out_part = lax.dot_general(
        branch_hidden, d_branch, (((0,), (0,)), ((), ())), preferred_element_type=jnp.float32
    )
    hidden_f = branch_hidden.astype(jnp.float32)
    d_pre = (
        lax.dot_general(
            d_branch, branch_out, (((1,), (1,)), ((), ())), preferred_element_type=jnp.float32
        )
        * (1.0 - hidden_f * hidden_f)
    ).astype(jnp.bfloat16)
    grad_in_part = lax.dot_general(
        sensor_values, d_pre, (((0,), (0,)), ((), ())), preferred_element_type=jnp.float32
    )
    own_rows = hidden_own.shape[0] * 4
    d_tangents = lax.psum_scatter(
        lax.dot_general(
            cotangent, branch_feat, (((0,), (0,)), ((), ())), preferred_element_type=jnp.float32
        ),
        "fn",
        scatter_dimension=0,
        tiled=True,
    )
    hidden_rows = hidden_own.reshape(own_rows, trunk_width)
    grad_trunk_part = trunk_weight_grad(hidden_rows, d_tangents)
    grad_branch_in, grad_branch_out, grad_trunk_out = (
        lax.psum_scatter(grad_in_part, "fn", scatter_dimension=0, tiled=True),
        lax.psum_scatter(grad_out_part, "fn", scatter_dimension=0, tiled=True),
        lax.psum_scatter(grad_trunk_part, "fn", scatter_dimension=0, tiled=True),
    )
    return (grad_branch_in, grad_branch_out, grad_trunk_out)


def solution(mesh):
    return jax.shard_map(
        per_device,
        mesh=mesh,
        in_specs=(
            P(("ens", "fn"), None),
            P(("ens", "fn")),
            P(("ens", "fn"), None),
            P(("ens", "fn"), None),
            P(("ens", "fn")),
            P(),
            P(),
            P(),
            P(),
            P(),
            P(),
            P(),
            P(),
        ),
        out_specs=(P(("ens", "fn"), None), P(("ens", "fn"), None), P(("ens", "fn"), None)),
        check_vma=False,
    )
```

profile of v0, /device:TPU:0, one launch (start us, length us, event | category | flops | bytes accessed | tf_op | source)
XLA Modules:
  0.0 342.3 jit_solution(5720239062144035112)
XLA Ops:
  7.3 1.3 dynamic-slice
  9.3 0.9 dynamic-update-slice
  10.1 34.9 %all-reduce = bf16[128]{0:T(256)(128)(2,1)S(1)} all-reduce(bf16[128]{0:T(256)(128)(2,1)S(1)} %dynamic-update-slice), channel_id=1, replica_groups=mesh['ens'=2,'fn'=16] {'fn'}, use_global_device_ids=true, to_apply=%add | all-reduce | flops 128 | bytes 512
  45.1 0.7 add_multiply_fusion
  45.8 0.8 convert_multiply_fusion.1
  46.5 0.8 fusion.34
  47.3 17.0 %all-gather = bf16[16,8,2]{1,2,0:T(2,128)(2,1)S(1)} all-gather(bf16[1,8,2]{1,2,0:T(2,128)(2,1)S(1)} %get-tuple-element.31), channel_id=1, replica_groups=mesh['ens'=2,'fn'=16] {'fn'}, dimensions={0}, use_global_device_ids=true | all-gather | bytes 544 | tf_op jit(solution)/shard_map/all_gather | solution.py:113
  64.4 0.1 copy.29
  64.5 0.1 reshape.1204
  64.6 0.8 broadcast_multiply_fusion
  65.3 0.8 add_tanh_fusion
  66.1 1.2 fusion.5
  67.3 20.6 %all_gather.9 = bf16[128,4,512]{2,0,1:T(8,128)(2,1)S(1)} all-gather(bf16[8,4,512]{2,0,1:T(8,128)(2,1)S(1)} %fusion.5), channel_id=1, replica_groups=mesh['ens'=2,'fn'=16] {'fn'}, dimensions={0}, use_global_device_ids=true | all-gather | bytes 557056 | tf_op jit(solution)/shard_map/all_gather | solution.py:112
  88.0 1.5 fusion.1
  89.5 0.3 fusion.2
  89.8 0.3 fusion.10
  90.1 1.3 negate_multiply_fusion.1
  91.4 1.0 negate_multiply_fusion
  92.5 0.2 copy.32
  92.8 1.3 fusion.36
  94.1 0.3 fusion.4
  94.4 0.7 copy-done.1
  95.1 1.3 fusion.35
  96.6 52.3 %reduce-scatter.9.cloned.1.call-done = f32[32,512]{1,0:T(8,128)} async-done(((f32[512,512]{1,0:T(8,128)}), f32[32,512]{1,0:T(8,128)}) %reduce-scatter.9.cloned.1.call-update) | async-done | bytes 65552 | tf_op jit(solution)/shard_map/reduce_scatter | solution.py:139
  148.9 0.8 convert_element_type.84
  149.8 0.3 fusion.37
  150.1 2.1 convolution_add_fusion
  152.3 2.1 convolution_bitcast_fusion
  154.4 1.9 copy.35
  156.3 53.7 %reduce-scatter.7.cloned.1.call-done = f32[32,512]{1,0:T(8,128)} async-done(((f32[512,512]{1,0:T(8,128)}), f32[32,512]{1,0:T(8,128)}) %reduce-scatter.7.cloned.1.call-update) | async-done | bytes 65552 | tf_op jit(solution)/shard_map/reduce_scatter | solution.py:151
  210.0 60.6 %reduce-scatter.11.cloned.1.call-done = f32[32,512]{1,0:T(8,128)} async-done(((f32[512,512]{1,0:T(8,128)}), f32[32,512]{1,0:T(8,128)}) %reduce-scatter.11.cloned.1.call-update) | async-done | bytes 65552 | tf_op jit(solution)/shard_map/reduce_scatter | solution.py:152
  270.6 65.2 %reduce-scatter.13.cloned.1.call-done = f32[64,512]{1,0:T(8,128)} async-done(((f32[1024,512]{1,0:T(8,128)}), f32[64,512]{1,0:T(8,128)}) %reduce-scatter.13.cloned.1.call-update) | async-done | bytes 131088
  (28 shorter events, 0.5 us)
Async XLA Ops:
  7.2 80.8 %copy-start = (bf16[1024,512]{1,0:T(8,128)(2,1)S(1)}, bf16[1024,512]{1,0:T(8,128)(2,1)}, u32[]{:S(2)}) copy-start(bf16[1024,512]{1,0:T(8,128)(2,1)} %param.18) | copy-start | bytes 3145732
  7.2 82.3 %copy-start.2 = (bf16[512,512]{1,0:T(8,128)(2,1)S(1)}, bf16[512,512]{1,0:T(8,128)(2,1)}, u32[]{:S(2)}) copy-start(bf16[512,512]{1,0:T(8,128)(2,1)} %param.20) | copy-start | bytes 1572868
  7.2 82.3 %copy-start.4 = (f32[512]{0:T(512)S(1)}, f32[512]{0:T(512)}, u32[]{:S(2)}) copy-start(f32[512]{0:T(512)} %param.21) | copy-start | bytes 6148
  7.2 141.7 %reduce-scatter.9.cloned.1.call-start = ((), (), s32[]{:S(2)}) async-start(), calls=%async_computation.5 | async-start | bytes 1114112 | tf_op jit(solution)/shard_map/reduce_scatter | solution.py:139
  88.0 2.2 copy-start.3
  94.1 115.9 %reduce-scatter.7.cloned.1.call-start = ((), (), s32[]{:S(2)}) async-start(), calls=%async_computation.4 | async-start | bytes 1114112 | tf_op jit(solution)/shard_map/reduce_scatter | solution.py:151
  94.4 0.7 copy-start.1
  96.5 174.1 %reduce-scatter.11.cloned.1.call-start = ((), (), s32[]{:S(2)}) async-start(), calls=%async_computation.6 | async-start | bytes 1114112 | tf_op jit(solution)/shard_map/reduce_scatter | solution.py:152
  152.3 183.5 %reduce-scatter.13.cloned.1.call-start = ((), (), s32[]{:S(2)}) async-start(), calls=%async_computation.7 | async-start | bytes 2228224
Sparse Core Ops, SparseCore 0:
  94.2 54.7 reduce-scatter.8
  153.6 56.3 reduce-scatter.6
  214.2 56.3 reduce-scatter.10
  275.2 60.5 reduce-scatter.12
where the time goes:
time: 343 us; the launch traced here: 342 us
  waiting for transfers between devices  232 us (68%)
  blocking collectives  72.6 us (21%)
  between operations  14.6 us (4%)
  matrix products  10.8 us (3%)
  other arithmetic  6.92 us (2%)
  local copies, waits for them, and re-layouts  5.36 us (2%)
    unnamed x5, waiting for transfers between devices  65.3 us
    reduce_scatter x1, waiting for transfers between devices, per_device(): lax.psum_scatter(grad_trunk_part, 'fn', scatter_dimension=0, tiled=True)  60.6 us
    reduce_scatter x1, waiting for transfers between devices, per_device(): lax.psum_scatter(grad_out_part, 'fn', scatter_dimension=0, tiled=True)  53.7 us
    reduce_scatter x1, waiting for transfers between devices, per_device(): lax.psum_scatter(lax.dot_general(cotangent, branch_feat, (((0,), (0,)), (...  52.3 us
    unnamed x1, blocking collectives  34.9 us
    all_gather x1, blocking collectives, per_device(): lax.all_gather(tangents_own, 'fn', axis=0, tiled=True)  20.6 us
    all_gather x1, blocking collectives, per_device(): lax.all_gather(own_coords.astype(jnp.bfloat16), 'fn', axis=0, tiled=True)  17 us
  transfers between devices with their start and end apart: 4, of which 4 were waited for; matrix products, arithmetic and copies ran while one was open for 3% of the time, Pallas kernels for 0%

commit v1 on v0

--- a/solution.py
+++ b/solution.py
@@ -1,11 +1,18 @@
+import functools
 import math
 
 import jax
 import jax.numpy as jnp
 from jax import lax
+from jax.experimental import pallas as pl
+from jax.experimental.pallas import tpu as pltpu
 from jax.sharding import PartitionSpec as P
 
 GRID = 128
+MODES = 5
+MESH = pl.DeviceIdType.MESH
+ROW_DIMS = (((0,), (0,)), ((), ()))
+COL_DIMS = (((1,), (1,)), ((), ()))
 
 
 def grid_coords(point_index):
@@ -154,9 +161,382 @@
     return (grad_branch_in, grad_branch_out, grad_trunk_out)
 
 
+def to_column(row, count):
+    rows = lax.broadcasted_iota(jnp.int32, (count, count), 0)
+    lanes = lax.broadcasted_iota(jnp.int32, (count, count), 1)
+    return jnp.sum(jnp.where(rows == lanes, row, 0.0), axis=1, keepdims=True)
+
+
+def spread_rows(row, lanes):
+    return jnp.broadcast_to(row, (lanes, row.shape[1])).T
+
+
+def pick_mode(modes, table):
+    picked = jnp.broadcast_to(table[0:1, :], modes.shape)
+    for mode in range(2, MODES + 1):
+        picked = jnp.where(modes == float(mode), table[mode - 1 : mode, :], picked)
+    return picked
+
+
+def step_kernel(
+    n,
+    sensors,
+    amplitude,
+    modes,
+    points,
+    forcing,
+    branch_in,
+    branch_in_bias,
+    branch_out,
+    branch_out_bias,
+    trunk_in,
+    trunk_in_bias,
+    trunk_out,
+    trunk_out_bias,
+    grad_in_ref,
+    grad_out_ref,
+    grad_trunk_ref,
+    pts,
+    hid,
+    tang,
+    part,
+    wide,
+    half_send,
+    half_keep,
+    quarter_send,
+    from_core,
+    from_y,
+    from_z,
+    pts_send,
+    pts_recv,
+    core_send,
+    core_recv,
+    y_send,
+    y_recv,
+    z_send,
+    z_recv,
+):
+    f32, bf16 = jnp.float32, jnp.bfloat16
+    me = lax.axis_index("fn")
+    nz = n // 4
+    core = lax.rem(me, 2)
+    y_at = lax.rem(me // 2, 2)
+    z_at = me // 4
+    other_core = me + 1 - 2 * core
+    other_y = me + 2 - 4 * y_at
+    own = points.shape[1]
+    npts = own * n
+    rows = from_z.shape[2]
+
+    barrier = pltpu.get_barrier_semaphore()
+    for k in range(1, n):
+        pl.semaphore_signal(
+            barrier, inc=1, device_id={"fn": lax.rem(me + k, n)}, device_id_type=MESH
+        )
+
+    coords = (points[...].astype(f32) + 0.5) / GRID
+    lane = lax.broadcasted_iota(jnp.int32, (own, 128), 1)
+    pts[me] = jnp.where(
+        lane == 0,
+        to_column(coords[0:1, :], own),
+        jnp.where(
+            lane == 1,
+            to_column(coords[1:2, :], own),
+            to_column(forcing[...].astype(f32), own),
+        ),
+    )
+    hidden = jnp.tanh(
+        jnp.dot(sensors[...], branch_in[...], preferred_element_type=f32) + branch_in_bias[...]
+    ).astype(bf16)
+
+    pl.semaphore_wait(barrier, n - 1)
+
+    def points_copy(k):
+        return pltpu.make_async_remote_copy(
+            src_ref=pts.at[me],
+            dst_ref=pts.at[me],
+            send_sem=pts_send.at[k - 1],
+            recv_sem=pts_recv.at[k - 1],
+            device_id={"fn": lax.rem(me + k, n)},
+            device_id_type=MESH,
+        )
+
+    def points_arrival(k):
+        source = lax.rem(me + n - k, n)
+        return pltpu.make_async_remote_copy(
+            src_ref=pts.at[source],
+            dst_ref=pts.at[source],
+            send_sem=pts_send.at[k - 1],
+            recv_sem=pts_recv.at[k - 1],
+            device_id={"fn": source},
+            device_id_type=MESH,
+        )
+
+    for k in range(1, n):
+        points_copy(k).start()
+
+    feat = (
+        jnp.dot(hidden, branch_out[...], preferred_element_type=f32) + branch_out_bias[...]
+    ).astype(bf16)
+    fields = feat.shape[0]
+    amp = spread_rows(amplitude[...], npts)
+    mode_x = spread_rows(modes[0:1, :].astype(f32), npts)
+    mode_y = spread_rows(modes[1:2, :].astype(f32), npts)
+
+    for k in range(1, n):
+        points_arrival(k).wait_recv()
+    columns = pts[...].reshape(npts, 128)
+    lines = columns.T
+    x_row, y_row, force_row = lines[0:1, :], lines[1:2, :], lines[2:3, :]
+
+    weight_x, weight_y = trunk_in[0:1, :], trunk_in[1:2, :]
+    act = jnp.tanh(columns[:, 0:1] * weight_x + columns[:, 1:2] * weight_y + trunk_in_bias[...])
+    first = 1.0 - act * act
+    second = -2.0 * act * first
+    hid[0:npts, :] = act.astype(bf16)
+    hid[npts : 2 * npts, :] = (first * weight_x).astype(bf16)
+    hid[2 * npts : 3 * npts, :] = (first * weight_y).astype(bf16)
+    hid[3 * npts : 4 * npts, :] = (
+        second * (weight_x * weight_x + weight_y * weight_y)
+    ).astype(bf16)
+    flat = jnp.dot(hid[...], trunk_out[...], preferred_element_type=f32)
+    tang[0:npts, :] = (flat[0:npts, :] + trunk_out_bias[...]).astype(bf16)
+    tang[npts:, :] = flat[npts:, :].astype(bf16)
+
+    tile = lax.dot_general(feat, tang[...], COL_DIMS, preferred_element_type=f32)
+
+    freqs = (lax.broadcasted_iota(jnp.int32, (8, npts), 0) + 1).astype(f32) * math.pi
+    sin_x = pick_mode(mode_x, jnp.sin(freqs * x_row))
+    cos_x = pick_mode(mode_x, jnp.cos(freqs * x_row))
+    sin_y = pick_mode(mode_y, jnp.sin(freqs * y_row))
+    cos_y = pick_mode(mode_y, jnp.cos(freqs * y_row))
+    perm = jnp.exp(amp * sin_x * sin_y)
+    perm_dx = perm * amp * (mode_x * math.pi) * cos_x * sin_y
+    perm_dy = perm * amp * (mode_y * math.pi) * sin_x * cos_y
+    residual = (
+        tile[:, 0:npts]
+        - (
+            perm * tile[:, 3 * npts :]
+            + perm_dx * tile[:, npts : 2 * npts]
+            + perm_dy * tile[:, 2 * npts : 3 * npts]
+        )
+        - force_row
+    )
+    scaled = residual / npts
+    cot = jnp.concatenate(
+        [
+            scaled.astype(bf16),
+            (-scaled * perm_dx).astype(bf16),
+            (-scaled * perm_dy).astype(bf16),
+            (-scaled * perm).astype(bf16),
+        ],
+        axis=1,
+    )
+
+    def keep(piece, value, chunk, start):
+        for d in range(n):
+            at = (d % 2) * (n // 2) + ((d // 2) % 2) * nz + d // 4
+            block = value[d * chunk + start : d * chunk + start + rows, :]
+            wide[piece, at] = block
+            part[piece, at] = block.astype(bf16)
+
+    def core_copy(piece):
+        return pltpu.make_async_remote_copy(
+            src_ref=part.at[piece, pl.ds((1 - core) * (n // 2), n // 2)],
+            dst_ref=from_core.at[piece],
+            send_sem=core_send.at[piece],
+            recv_sem=core_recv.at[piece],
+            device_id={"fn": other_core},
+            device_id_type=MESH,
+        )
+
+    def y_copy(piece):
+        return pltpu.make_async_remote_copy(
+            src_ref=half_send.at[piece],
+            dst_ref=from_y.at[piece],
+            send_sem=y_send.at[piece],
+            recv_sem=y_recv.at[piece],
+            device_id={"fn": other_y},
+            device_id_type=MESH,
+        )
+
+    def z_copy(piece, k):
+        return pltpu.make_async_remote_copy(
+            src_ref=quarter_send.at[piece, k - 1],
+            dst_ref=from_z.at[piece, k - 1],
+            send_sem=z_send.at[piece, k - 1],
+            recv_sem=z_recv.at[piece, k - 1],
+            device_id={"fn": lax.rem(me + 4 * k, n)},
+            device_id_type=MESH,
+        )
+
+    def core_to_y(piece):
+        core_copy(piece).wait_recv()
+        away = (1 - y_at) * nz
+        half_send[piece] = (
+            wide[piece, pl.ds(core * (n // 2) + away, nz)]
+            + from_core[piece, pl.ds(away, nz)].astype(f32)
+        ).astype(bf16)
+        y_copy(piece).start()
+        half_keep[piece] = wide[piece, pl.ds(core * (n // 2) + y_at * nz, nz)] + from_core[
+            piece, pl.ds(y_at * nz, nz)
+        ].astype(f32)
+
+    def y_to_z(piece):
+        y_copy(piece).wait_recv()
+        for k in range(1, nz):
+            target = lax.rem(z_at + k, nz)
+            quarter_send[piece, k - 1] = (
+                half_keep[piece, target] + from_y[piece, target].astype(f32)
+            ).astype(bf16)
+            z_copy(piece, k).start()
+
+    def finish(piece):
+        total = half_keep[piece, z_at] + from_y[piece, z_at].astype(f32)
+        for k in range(1, nz):
+            z_copy(piece, k).wait_recv()
+            total = total + from_z[piece, k - 1].astype(f32)
+        return total
+
+    trunk_mix = jnp.dot(cot, hid[...], preferred_element_type=f32)
+    upper = trunk_mix.astype(bf16)
+    lower = (trunk_mix - upper.astype(f32)).astype(bf16)
+    grad_trunk = lax.dot_general(
+        upper, feat, ROW_DIMS, preferred_element_type=f32
+    ) + lax.dot_general(lower, feat, ROW_DIMS, preferred_element_type=f32)
+    keep(0, grad_trunk, rows, 0)
+    core_copy(0).start()
+
+    d_branch = jnp.dot(cot, tang[...], preferred_element_type=f32).astype(bf16)
+    keep(1, lax.dot_general(hidden, d_branch, ROW_DIMS, preferred_element_type=f32), rows, 0)
+    core_copy(1).start()
+    core_to_y(0)
+
+    hidden_f = hidden.astype(f32)
+    d_pre = (
+        lax.dot_general(d_branch, branch_out[...], COL_DIMS, preferred_element_type=f32)
+        * (1.0 - hidden_f * hidden_f)
+    ).astype(bf16)
+    grad_in = lax.dot_general(sensors[...], d_pre, ROW_DIMS, preferred_element_type=f32)
+    core_to_y(1)
+    keep(2, grad_in, 2 * rows, 0)
+    core_copy(2).start()
+    keep(3, grad_in, 2 * rows, rows)
+    core_copy(3).start()
+    y_to_z(0)
+    core_to_y(2)
+    core_to_y(3)
+    y_to_z(1)
+    y_to_z(2)
+    y_to_z(3)
+    grad_trunk_ref[...] = finish(0)
+    grad_out_ref[...] = finish(1)
+    grad_in_ref[0:rows, :] = finish(2)
+    grad_in_ref[rows : 2 * rows, :] = finish(3)
+
+    for k in range(1, n):
+        points_copy(k).wait_send()
+    for piece in range(4):
+        core_copy(piece).wait_send()
+        y_copy(piece).wait_send()
+        for k in range(1, nz):
+            z_copy(piece, k).wait_send()
+
+
+def fused_step(
+    n,
+    sensor_values,
+    amplitude,
+    field_modes,
+    point_index,
+    forcing,
+    branch_in,
+    branch_in_bias,
+    branch_out,
+    branch_out_bias,
+    trunk_in,
+    trunk_in_bias,
+    trunk_out,
+    trunk_out_bias,
+):
+    f32, bf16 = jnp.float32, jnp.bfloat16
+    sensors = sensor_values.shape[1]
+    width = trunk_out.shape[1]
+    npts = point_index.shape[0] * n
+    rows = width // n
+    nz = n // 4
+    row = lambda array: array.reshape(1, array.shape[0])
+    vmem = pl.BlockSpec(memory_space=pltpu.VMEM)
+    return pl.pallas_call(
+        functools.partial(step_kernel, n),
+        out_shape=(
+            jax.ShapeDtypeStruct((sensors // n, width), f32),
+            jax.ShapeDtypeStruct((rows, width), f32),
+            jax.ShapeDtypeStruct((rows, width), f32),
+        ),
+        in_specs=[vmem] * 13,
+        out_specs=(vmem, vmem, vmem),
+        scratch_shapes=[
+            pltpu.VMEM((n, point_index.shape[0], 128), f32),
+            pltpu.VMEM((4 * npts, width), bf16),
+            pltpu.VMEM((4 * npts, width), bf16),
+            pltpu.VMEM((4, n, rows, width), bf16),
+            pltpu.VMEM((4, n, rows, width), f32),
+            pltpu.VMEM((4, nz, rows, width), bf16),
+            pltpu.VMEM((4, nz, rows, width), f32),
+            pltpu.VMEM((4, nz - 1, rows, width), bf16),
+            pltpu.VMEM((4, n // 2, rows, width), bf16),
+            pltpu.VMEM((4, nz, rows, width), bf16),
+            pltpu.VMEM((4, nz - 1, rows, width), bf16),
+            pltpu.SemaphoreType.DMA((n - 1,)),
+            pltpu.SemaphoreType.DMA((n - 1,)),
+            pltpu.SemaphoreType.DMA((4,)),
+            pltpu.SemaphoreType.DMA((4,)),
+            pltpu.SemaphoreType.DMA((4,)),
+            pltpu.SemaphoreType.DMA((4,)),
+            pltpu.SemaphoreType.DMA((4, nz - 1)),
+            pltpu.SemaphoreType.DMA((4, nz - 1)),
+        ],
+        compiler_params=pltpu.CompilerParams(
+            collective_id=0, has_side_effects=True, vmem_limit_bytes=48 * 2**20
+        ),
+    )(
+        sensor_values,
+        row(amplitude),
+        field_modes.T,
+        point_index.T,
+        row(forcing),
+        branch_in,
+        row(branch_in_bias),
+        branch_out,
+        row(branch_out_bias),
+        trunk_in,
+        row(trunk_in_bias),
+        trunk_out,
+        row(trunk_out_bias),
+    )
+
+
+def device_step(n, *arrays):
+    sensor_values, point_index, trunk_out = arrays[0], arrays[3], arrays[11]
+    rows = trunk_out.shape[1] // n
+    fits = (
+        n % 4 == 0
+        and n >= 8
+        and rows % 16 == 0
+        and point_index.shape[0] == 8
+        and point_index.shape[0] * n == 128
+        and sensor_values.shape[1] == 2 * rows * n
+        and trunk_out.shape[0] == trunk_out.shape[1]
+    )
+    if fits:
+        return fused_step(n, *arrays)
+    return per_device(*arrays)
+
+
 def solution(mesh):
     return jax.shard_map(
-        per_device,
+        functools.partial(device_step, mesh.shape["fn"]),
         mesh=mesh,
         in_specs=(
             P(("ens", "fn"), None),

time: 343 us -> 40.8 us (0.12)
  waiting for transfers between devices: 232 us -> 0 us
  blocking collectives: 72.6 us -> 0 us
  Pallas kernels: 0 us -> 31.4 us
  between operations: 14.6 us -> 0.71 us
  matrix products: 10.8 us -> 0 us
  other arithmetic: 6.92 us -> 0 us
    reduce_scatter x3 -> x0, waiting for transfers between devices: 167 us -> none  [the longest x1 60.6 us: per_device(): lax.psum_scatter(grad_trunk_part, 'fn', scatter_dimension=0, tiled=True)]
    unnamed x5 -> x0, waiting for transfers between devices: 65.3 us -> none
    all_gather x2 -> x0, blocking collectives: 37.6 us -> none  [the longest x1 20.6 us: per_device(): lax.all_gather(tangents_own, 'fn', axis=0, tiled=True)]
    unnamed x1 -> x0, blocking collectives: 34.9 us -> none
    pallas_call x0 -> x1, Pallas kernels: none -> 31.4 us  [fused_step(): pl.pallas_call(functools.partial(step_kernel, n), out_shape=(jax.ShapeDty...]
    dot_general x10 -> x0, matrix products: 10.8 us -> none  [the longest x1 2.15 us: trunk_weight_grad(): lax.dot_general(hidden_rows, lower_part, dims, preferred_element_type=jnp...]
    mul x4 -> x0, other arithmetic: 3.8 us -> none  [the longest x1 1.25 us: tile_cotangent(): -scaled * perm_dx]
    unnamed x14 -> x29, local copies, waits for them, and re-layouts: 4.79 us -> 8.31 us
  transfers between devices with their start and end apart: 4 -> 0, of which waited for: 4 -> 0; matrix products, arithmetic and copies ran while one was open for 3% -> 0% of each run, Pallas kernels for 0% -> 0%
where the time goes in v1:
time: 40.8 us; the launch traced here: 40.4 us
  Pallas kernels  31.4 us (77%)
  local copies, waits for them, and re-layouts  8.31 us (20%)
  between operations  0.71 us (2%)
    pallas_call x1, Pallas kernels, fused_step(): pl.pallas_call(functools.partial(step_kernel, n), out_shape=(jax.ShapeDty...  31.4 us
    unnamed x29, local copies, waits for them, and re-layouts  8.31 us

profile of v1, /device:TPU:0, one launch (start us, length us, event | category | flops | bytes accessed | tf_op | source)
XLA Modules:
  0.0 40.4 jit_solution(11385747513746201590)
XLA Ops:
  0.6 0.0 copy-start.9
  0.6 0.0 copy-start.8
  0.7 0.0 copy-start.7
  0.7 0.0 copy-start.6
  0.7 0.0 copy-start.4
  0.7 0.0 copy-start.5
  0.7 0.0 copy-start.10
  0.7 0.6 %copy-done.9 = f32[512]{0:T(512)S(1)} copy-done((f32[512]{0:T(512)S(1)}, f32[512]{0:T(512)}, u32[]{:S(2)}) %copy-start.9) | copy-done | bytes 2072
  1.3 0.0 copy-done.8
  1.3 0.0 copy-done.7
  1.4 0.0 copy-done.6
  1.4 0.0 copy-done.4
  1.4 0.0 copy-done.5
  1.4 0.0 copy-done.10
  1.4 0.0 copy-start
  1.4 1.2 %copy-done = bf16[1024,512]{1,0:T(8,128)(2,1)S(1)} copy-done((bf16[1024,512]{1,0:T(8,128)(2,1)S(1)}, bf16[1024,512]{1,0:T(8,128)(2,1)}, u32[]{:S(2)}) %copy-start) | copy-done | bytes 1048600
  2.6 0.0 copy-start.1
  2.6 1.0 %copy-done.1 = bf16[256,1024]{1,0:T(8,128)(2,1)S(1)} copy-done((bf16[256,1024]{1,0:T(8,128)(2,1)S(1)}, bf16[256,1024]{1,0:T(8,128)(2,1)}, u32[]{:S(2)}) %copy-start.1) | copy-done | bytes 524312
  3.7 0.0 copy-start.2
  3.7 1.0 %copy-done.2 = bf16[512,512]{1,0:T(8,128)(2,1)S(1)} copy-done((bf16[512,512]{1,0:T(8,128)(2,1)S(1)}, bf16[512,512]{1,0:T(8,128)(2,1)}, u32[]{:S(2)}) %copy-start.2) | copy-done | bytes 524312
  4.7 0.0 copy-start.3
  4.7 1.0 %copy-done.3 = bf16[512,512]{1,0:T(8,128)(2,1)S(1)} copy-done((bf16[512,512]{1,0:T(8,128)(2,1)S(1)}, bf16[512,512]{1,0:T(8,128)(2,1)}, u32[]{:S(2)}) %copy-start.3) | copy-done | bytes 524312
  5.8 0.0 copy-start.11
  5.8 0.7 %copy-done.11 = s32[8,2]{0,1:T(2,128)S(1)} copy-done((s32[8,2]{0,1:T(2,128)S(1)}, s32[8,2]{0,1:T(2,128)}, u32[]{:S(2)}) %copy-start.11) | copy-done | bytes 88
  6.4 0.0 copy-start.12
  6.4 0.7 %copy-done.12 = bf16[8]{0:T(256)(128)(2,1)S(1)} copy-done((bf16[8]{0:T(256)(128)(2,1)S(1)}, bf16[8]{0:T(256)(128)(2,1)}, u32[]{:S(2)}) %copy-start.12) | copy-done | bytes 40
  7.1 31.4 %shard_map.148 = (f32[64,512]{1,0:T(8,128)S(1)}, f32[32,512]{1,0:T(8,128)S(1)}, f32[32,512]{1,0:T(8,128)S(1)}) custom-call(bf16[256,1024]{1,0:T(8,128)(2,1)S(1)} %copy-done.1, f32[1,256]{1,0:T(1,128)S(1)} %bitcast.13, s32[2,256]{1,0:T(2,128)S(1)} %bitcast.8, s32[2,8]{1,0:T(2,128)S(1)} %bitcast.14, bf16[1,8]{1,0:T(2,128)(2,1)S(1)} %bitcast.15, ...), custom_call_target="tpu_custom_call" | custom-call | tf_op jit(solution)/shard_map/pallas_call | solution.py:470
  38.5 0.7 %copy.19 = f32[64,512]{1,0:T(8,128)} copy(f32[64,512]{1,0:T(8,128)S(1)} %get-tuple-element.6) | data formatting | bytes 262144
  39.2 0.6 %copy.20 = f32[32,512]{1,0:T(8,128)} copy(f32[32,512]{1,0:T(8,128)S(1)} %get-tuple-element.7) | data formatting | bytes 131072
  39.8 0.6 %copy.21 = f32[32,512]{1,0:T(8,128)} copy(f32[32,512]{1,0:T(8,128)S(1)} %get-tuple-element.8) | data formatting | bytes 131072
Async XLA Ops:
  0.6 0.7 %copy-start.9 = (f32[512]{0:T(512)S(1)}, f32[512]{0:T(512)}, u32[]{:S(2)}) copy-start(f32[512]{0:T(512)} %param.25) | copy-start | bytes 6148
  0.6 0.7 %copy-start.8 = (f32[512]{0:T(512)S(1)}, f32[512]{0:T(512)}, u32[]{:S(2)}) copy-start(f32[512]{0:T(512)} %param.23) | copy-start | bytes 6148
  0.7 0.7 %copy-start.7 = (f32[512]{0:T(512)S(1)}, f32[512]{0:T(512)}, u32[]{:S(2)}) copy-start(f32[512]{0:T(512)} %param.21) | copy-start | bytes 6148
  0.7 0.7 %copy-start.6 = (f32[512]{0:T(512)S(1)}, f32[512]{0:T(512)}, u32[]{:S(2)}) copy-start(f32[512]{0:T(512)} %param.19) | copy-start | bytes 6148
  0.7 0.7 %copy-start.4 = (f32[2,512]{1,0:T(2,128)S(1)}, f32[2,512]{1,0:T(2,128)}, u32[]{:S(2)}) copy-start(f32[2,512]{1,0:T(2,128)} %trunk_in.1) | copy-start | bytes 12292
  0.7 0.7 %copy-start.5 = (s32[256,2]{0,1:T(2,128)S(1)}, s32[256,2]{0,1:T(2,128)}, u32[]{:S(2)}) copy-start(s32[256,2]{0,1:T(2,128)} %param.15) | copy-start | bytes 6148
  0.7 0.7 %copy-start.10 = (f32[256]{0:T(256)S(1)}, f32[256]{0:T(256)}, u32[]{:S(2)}) copy-start(f32[256]{0:T(256)} %param.14) | copy-start | bytes 3076
  1.4 1.2 %copy-start = (bf16[1024,512]{1,0:T(8,128)(2,1)S(1)}, bf16[1024,512]{1,0:T(8,128)(2,1)}, u32[]{:S(2)}) copy-start(bf16[1024,512]{1,0:T(8,128)(2,1)} %branch_in.1) | copy-start | bytes 3145732
  2.6 1.0 %copy-start.1 = (bf16[256,1024]{1,0:T(8,128)(2,1)S(1)}, bf16[256,1024]{1,0:T(8,128)(2,1)}, u32[]{:S(2)}) copy-start(bf16[256,1024]{1,0:T(8,128)(2,1)} %sensors.1) | copy-start | bytes 1572868
  3.7 1.0 %copy-start.2 = (bf16[512,512]{1,0:T(8,128)(2,1)S(1)}, bf16[512,512]{1,0:T(8,128)(2,1)}, u32[]{:S(2)}) copy-start(bf16[512,512]{1,0:T(8,128)(2,1)} %branch_out.1) | copy-start | bytes 1572868
  4.7 1.0 %copy-start.3 = (bf16[512,512]{1,0:T(8,128)(2,1)S(1)}, bf16[512,512]{1,0:T(8,128)(2,1)}, u32[]{:S(2)}) copy-start(bf16[512,512]{1,0:T(8,128)(2,1)} %trunk_out.1) | copy-start | bytes 1572868
  5.8 0.7 %copy-start.11 = (s32[8,2]{0,1:T(2,128)S(1)}, s32[8,2]{0,1:T(2,128)}, u32[]{:S(2)}) copy-start(s32[8,2]{0,1:T(2,128)} %param.16) | copy-start | bytes 196
  6.4 0.7 %copy-start.12 = (bf16[8]{0:T(256)(128)(2,1)S(1)}, bf16[8]{0:T(256)(128)(2,1)}, u32[]{:S(2)}) copy-start(bf16[8]{0:T(256)(128)(2,1)} %param.17) | copy-start | bytes 52

commit v2 on v1

--- a/solution.py
+++ b/solution.py
@@ -10,6 +10,7 @@
 
 GRID = 128
 MODES = 5
+PIECE = 16
 MESH = pl.DeviceIdType.MESH
 ROW_DIMS = (((0,), (0,)), ((), ()))
 COL_DIMS = (((1,), (1,)), ((), ()))
@@ -178,44 +179,47 @@
     return picked
 
 
-def step_kernel(
-    n,
-    sensors,
-    amplitude,
-    modes,
-    points,
-    forcing,
-    branch_in,
-    branch_in_bias,
-    branch_out,
-    branch_out_bias,
-    trunk_in,
-    trunk_in_bias,
-    trunk_out,
-    trunk_out_bias,
-    grad_in_ref,
-    grad_out_ref,
-    grad_trunk_ref,
-    pts,
-    hid,
-    tang,
-    part,
-    wide,
-    half_send,
-    half_keep,
-    quarter_send,
-    from_core,
-    from_y,
-    from_z,
-    pts_send,
-    pts_recv,
-    core_send,
-    core_recv,
-    y_send,
-    y_recv,
-    z_send,
-    z_recv,
-):
+def step_kernel(n, *refs):
+    hbm, refs = refs[:13], refs[13:]
+    out_ref, refs = refs[0], refs[1:]
+    staged, refs = refs[:13], refs[13:]
+    (
+        sensors,
+        amplitude,
+        modes,
+        points,
+        forcing,
+        branch_in,
+        branch_in_bias,
+        branch_out,
+        branch_out_bias,
+        trunk_in,
+        trunk_in_bias,
+        trunk_out,
+        trunk_out_bias,
+    ) = staged
+    (
+        pts,
+        hid,
+        tang,
+        part,
+        wide,
+        half_send,
+        half_keep,
+        quarter_send,
+        from_core,
+        from_y,
+        from_z,
+        load_sem,
+        pts_send,
+        pts_recv,
+        core_send,
+        core_recv,
+        y_send,
+        y_recv,
+        z_send,
+        z_recv,
+    ) = refs
     f32, bf16 = jnp.float32, jnp.bfloat16
     me = lax.axis_index("fn")
     nz = n // 4
@@ -227,6 +231,7 @@
     own = points.shape[1]
     npts = own * n
     rows = from_z.shape[2]
+    out_rows = out_ref.shape[0] // 4
 
     barrier = pltpu.get_barrier_semaphore()
     for k in range(1, n):
@@ -234,6 +239,12 @@
             barrier, inc=1, device_id={"fn": lax.rem(me + k, n)}, device_id_type=MESH
         )
 
+    loads = [pltpu.make_async_copy(hbm[i], staged[i], load_sem.at[i]) for i in range(13)]
+    for i in (3, 4, 0, 5, 6, 7, 8, 1, 2, 9, 10, 11, 12):
+        loads[i].start()
+
+    loads[3].wait()
+    loads[4].wait()
     coords = (points[...].astype(f32) + 0.5) / GRID
     lane = lax.broadcasted_iota(jnp.int32, (own, 128), 1)
     pts[me] = jnp.where(
@@ -245,10 +256,6 @@
             to_column(forcing[...].astype(f32), own),
         ),
     )
-    hidden = jnp.tanh(
-        jnp.dot(sensors[...], branch_in[...], preferred_element_type=f32) + branch_in_bias[...]
-    ).astype(bf16)
-
     pl.semaphore_wait(barrier, n - 1)
 
     def points_copy(k):
@@ -272,9 +279,17 @@
             device_id_type=MESH,
         )
 
-    for k in range(1, n):
+    for k in far_first(n):
         points_copy(k).start()
 
+    for i in (0, 5, 6):
+        loads[i].wait()
+    hidden = jnp.tanh(
+        jnp.dot(sensors[...], branch_in[...], preferred_element_type=f32) + branch_in_bias[...]
+    ).astype(bf16)
+
+    for i in (7, 8, 1, 2):
+        loads[i].wait()
     feat = (
         jnp.dot(hidden, branch_out[...], preferred_element_type=f32) + branch_out_bias[...]
     ).astype(bf16)
@@ -283,6 +298,8 @@
     mode_x = spread_rows(modes[0:1, :].astype(f32), npts)
     mode_y = spread_rows(modes[1:2, :].astype(f32), npts)
 
+    for i in (9, 10, 11, 12):
+        loads[i].wait()
     for k in range(1, n):
         points_arrival(k).wait_recv()
     columns = pts[...].reshape(npts, 128)
@@ -398,49 +415,70 @@
             total = total + from_z[piece, k - 1].astype(f32)
         return total
 
-    trunk_mix = jnp.dot(cot, hid[...], preferred_element_type=f32)
-    upper = trunk_mix.astype(bf16)
-    lower = (trunk_mix - upper.astype(f32)).astype(bf16)
-    grad_trunk = lax.dot_general(
-        upper, feat, ROW_DIMS, preferred_element_type=f32
-    ) + lax.dot_general(lower, feat, ROW_DIMS, preferred_element_type=f32)
-    keep(0, grad_trunk, rows, 0)
-    core_copy(0).start()
-
+    unit = out_rows // rows
     d_branch = jnp.dot(cot, tang[...], preferred_element_type=f32).astype(bf16)
-    keep(1, lax.dot_general(hidden, d_branch, ROW_DIMS, preferred_element_type=f32), rows, 0)
-    core_copy(1).start()
-    core_to_y(0)
+    grad_out = lax.dot_general(hidden, d_branch, ROW_DIMS, preferred_element_type=f32)
+    for i in range(unit):
+        keep(i, grad_out, out_rows, i * rows)
+        core_copy(i).start()
 
     hidden_f = hidden.astype(f32)
     d_pre = (
         lax.dot_general(d_branch, branch_out[...], COL_DIMS, preferred_element_type=f32)
         * (1.0 - hidden_f * hidden_f)
     ).astype(bf16)
+    for i in range(unit):
+        core_to_y(i)
     grad_in = lax.dot_general(sensors[...], d_pre, ROW_DIMS, preferred_element_type=f32)
-    core_to_y(1)
-    keep(2, grad_in, 2 * rows, 0)
-    core_copy(2).start()
-    keep(3, grad_in, 2 * rows, rows)
-    core_copy(3).start()
+    for i in range(2 * unit):
+        keep(unit + i, grad_in, 2 * out_rows, i * rows)
+        core_copy(unit + i).start()
+
+    trunk_mix = jnp.dot(cot, hid[...], preferred_element_type=f32)
+    upper = trunk_mix.astype(bf16)
+    lower = (trunk_mix - upper.astype(f32)).astype(bf16)
+    for i in range(unit):
+        core_to_y(unit + i)
+    grad_trunk = lax.dot_general(
+        upper, feat, ROW_DIMS, preferred_element_type=f32
+    ) + lax.dot_general(lower, feat, ROW_DIMS, preferred_element_type=f32)
+    for i in range(unit):
+        keep(3 * unit + i, grad_trunk, out_rows, i * rows)
+        core_copy(3 * unit + i).start()
     y_to_z(0)
-    core_to_y(2)
-    core_to_y(3)
-    y_to_z(1)
-    y_to_z(2)
-    y_to_z(3)
-    grad_trunk_ref[...] = finish(0)
-    grad_out_ref[...] = finish(1)
-    grad_in_ref[0:rows, :] = finish(2)
-    grad_in_ref[rows : 2 * rows, :] = finish(3)
+    for i in range(2 * unit, 4 * unit):
+        core_to_y(i)
+        y_to_z(i - 2 * unit + 1)
+    for i in range(2 * unit + 1, 4 * unit):
+        y_to_z(i)
+    for i in range(4 * unit):
+        out_ref[i * rows : (i + 1) * rows, :] = finish(i)
 
     for k in range(1, n):
         points_copy(k).wait_send()
-    for piece in range(4):
+    for piece in range(4 * unit):
         core_copy(piece).wait_send()
         y_copy(piece).wait_send()
         for k in range(1, nz):
             z_copy(piece, k).wait_send()
+
+
+def far_first(n):
+    return sorted(range(1, n), key=lambda k: -min(k, n - k))
+
+
+def split_kernel(sums, grad_in, grad_out, grad_trunk, sems):
+    rows = grad_out.shape[0]
+    moves = [
+        pltpu.make_async_copy(sums.at[pl.ds(start, out.shape[0])], out, sems.at[i])
+        for i, (start, out) in enumerate(
+            ((rows, grad_in), (0, grad_out), (3 * rows, grad_trunk))
+        )
+    ]
+    for move in moves:
+        move.start()
+    for move in moves:
+        move.wait()
 
 
 def fused_step(
@@ -460,47 +498,15 @@
     trunk_out_bias,
 ):
     f32, bf16 = jnp.float32, jnp.bfloat16
-    sensors = sensor_values.shape[1]
     width = trunk_out.shape[1]
-    npts = point_index.shape[0] * n
-    rows = width // n
+    own = point_index.shape[0]
+    npts = own * n
+    out_rows = width // n
+    rows = PIECE
+    pieces = 4 * out_rows // rows
     nz = n // 4
     row = lambda array: array.reshape(1, array.shape[0])
-    vmem = pl.BlockSpec(memory_space=pltpu.VMEM)
-    return pl.pallas_call(
-        functools.partial(step_kernel, n),
-        out_shape=(
-            jax.ShapeDtypeStruct((sensors // n, width), f32),
-            jax.ShapeDtypeStruct((rows, width), f32),
-            jax.ShapeDtypeStruct((rows, width), f32),
-        ),
-        in_specs=[vmem] * 13,
-        out_specs=(vmem, vmem, vmem),
-        scratch_shapes=[
-            pltpu.VMEM((n, point_index.shape[0], 128), f32),
-            pltpu.VMEM((4 * npts, width), bf16),
-            pltpu.VMEM((4 * npts, width), bf16),
-            pltpu.VMEM((4, n, rows, width), bf16),
-            pltpu.VMEM((4, n, rows, width), f32),
-            pltpu.VMEM((4, nz, rows, width), bf16),
-            pltpu.VMEM((4, nz, rows, width), f32),
-            pltpu.VMEM((4, nz - 1, rows, width), bf16),
-            pltpu.VMEM((4, n // 2, rows, width), bf16),
-            pltpu.VMEM((4, nz, rows, width), bf16),
-            pltpu.VMEM((4, nz - 1, rows, width), bf16),
-            pltpu.SemaphoreType.DMA((n - 1,)),
-            pltpu.SemaphoreType.DMA((n - 1,)),
-            pltpu.SemaphoreType.DMA((4,)),
-            pltpu.SemaphoreType.DMA((4,)),
-            pltpu.SemaphoreType.DMA((4,)),
-            pltpu.SemaphoreType.DMA((4,)),
-            pltpu.SemaphoreType.DMA((4, nz - 1)),
-            pltpu.SemaphoreType.DMA((4, nz - 1)),
-        ],
-        compiler_params=pltpu.CompilerParams(
-            collective_id=0, has_side_effects=True, vmem_limit_bytes=48 * 2**20
-        ),
-    )(
+    operands = (
         sensor_values,
         row(amplitude),
         field_modes.T,
@@ -515,6 +521,51 @@
         trunk_out,
         row(trunk_out_bias),
     )
+    hbm = pl.BlockSpec(memory_space=pl.ANY)
+    vmem = pl.BlockSpec(memory_space=pltpu.VMEM)
+    sums = pl.pallas_call(
+        functools.partial(step_kernel, n),
+        out_shape=jax.ShapeDtypeStruct((4 * out_rows, width), f32),
+        in_specs=[pl.BlockSpec(memory_space=pltpu.HBM)] * len(operands),
+        out_specs=vmem,
+        scratch_shapes=[pltpu.VMEM(array.shape, array.dtype) for array in operands]
+        + [
+            pltpu.VMEM((n, own, 128), f32),
+            pltpu.VMEM((4 * npts, width), bf16),
+            pltpu.VMEM((4 * npts, width), bf16),
+            pltpu.VMEM((pieces, n, rows, width), bf16),
+            pltpu.VMEM((pieces, n, rows, width), f32),
+            pltpu.VMEM((pieces, nz, rows, width), bf16),
+            pltpu.VMEM((pieces, nz, rows, width), f32),
+            pltpu.VMEM((pieces, nz - 1, rows, width), bf16),
+            pltpu.VMEM((pieces, n // 2, rows, width), bf16),
+            pltpu.VMEM((pieces, nz, rows, width), bf16),
+            pltpu.VMEM((pieces, nz - 1, rows, width), bf16),
+            pltpu.SemaphoreType.DMA((len(operands),)),
+            pltpu.SemaphoreType.DMA((n - 1,)),
+            pltpu.SemaphoreType.DMA((n - 1,)),
+            pltpu.SemaphoreType.DMA((pieces,)),
+            pltpu.SemaphoreType.DMA((pieces,)),
+            pltpu.SemaphoreType.DMA((pieces,)),
+            pltpu.SemaphoreType.DMA((pieces,)),
+            pltpu.SemaphoreType.DMA((pieces, nz - 1)),
+            pltpu.SemaphoreType.DMA((pieces, nz - 1)),
+        ],
+        compiler_params=pltpu.CompilerParams(
+            collective_id=0, has_side_effects=True, vmem_limit_bytes=60 * 2**20
+        ),
+    )(*operands)
+    return pl.pallas_call(
+        split_kernel,
+        out_shape=(
+            jax.ShapeDtypeStruct((2 * out_rows, width), f32),
+            jax.ShapeDtypeStruct((out_rows, width), f32),
+            jax.ShapeDtypeStruct((out_rows, width), f32),
+        ),
+        in_specs=[vmem],
+        out_specs=(hbm, hbm, hbm),
+        scratch_shapes=[pltpu.SemaphoreType.DMA((3,))],
+    )(sums)
 
 
 def device_step(n, *arrays):

time: 40.8 us -> 34.2 us (0.84)
  local copies, waits for them, and re-layouts: 8.31 us -> 0 us
  Pallas kernels: 31.4 us -> 33.4 us
    unnamed x29 -> x0, local copies, waits for them, and re-layouts: 8.31 us -> none
    pallas_call x1 -> x2, Pallas kernels: 31.4 us -> 33.4 us  [the longest x1 31.7 us: fused_step(): pl.pallas_call(functools.partial(step_kernel, n), out_shape=jax.ShapeDtyp...]
where the time goes in v2:
time: 34.2 us; the launch traced here: 34 us
  Pallas kernels  33.4 us (98%)
  between operations  0.64 us (2%)
    pallas_call x1, Pallas kernels, fused_step(): pl.pallas_call(functools.partial(step_kernel, n), out_shape=jax.ShapeDtyp...  31.7 us
    pallas_call x1, Pallas kernels, fused_step(): pl.pallas_call(split_kernel, out_shape=(jax.ShapeDtypeStruct((2 * out_row...  1.67 us

profile of v2, /device:TPU:0, one launch (start us, length us, event | category | flops | bytes accessed | tf_op | source)
XLA Modules:
  0.0 34.0 jit_solution(13724743422674862497)
XLA Ops:
  0.6 31.7 %shard_map.148.sums = f32[128,512]{1,0:T(8,128)} custom-call(bf16[256,1024]{1,0:T(8,128)(2,1)} %refs_0_.1, f32[1,256]{1,0:T(1,128)} %bitcast.13, s32[2,256]{1,0:T(2,128)} %bitcast.8, s32[2,8]{1,0:T(2,128)} %bitcast.14, bf16[1,8]{1,0:T(2,128)(2,1)} %bitcast.15, bf16[1024,512]{1,0:T(8,128)(2,1)} %refs_5_.1, f32[1,512]{1,0:T(1,128)} %bitcast.9, ...), custom_call_target="tpu_custom_call" | custom-call | tf_op jit(solution)/shard_map/pallas_call | solution.py:526
  32.3 1.7 %shard_map.149 = (f32[64,512]{1,0:T(8,128)}, f32[32,512]{1,0:T(8,128)}, f32[32,512]{1,0:T(8,128)}) custom-call(f32[128,512]{1,0:T(8,128)} %shard_map.148.sums), custom_call_target="tpu_custom_call" | custom-call | tf_op jit(solution)/shard_map/pallas_call | solution.py:558

commit v3 on v2

--- a/solution.py
+++ b/solution.py
@@ -11,6 +11,7 @@
 GRID = 128
 MODES = 5
 PIECE = 16
+Z_FIRST = (1, 2)
 MESH = pl.DeviceIdType.MESH
 ROW_DIMS = (((0,), (0,)), ((), ()))
 COL_DIMS = (((1,), (1,)), ((), ()))
@@ -210,6 +211,10 @@
         from_core,
         from_y,
         from_z,
+        lines_send,
+        from_lines,
+        last_send,
+        from_last,
         load_sem,
         pts_send,
         pts_recv,
@@ -387,7 +392,58 @@
             device_id_type=MESH,
         )
 
+    def line_copy(piece, k):
+        slot = Z_FIRST.index(piece)
+        return pltpu.make_async_remote_copy(
+            src_ref=lines_send.at[slot, k - 1],
+            dst_ref=from_lines.at[slot, k - 1],
+            send_sem=z_send.at[piece, k - 1],
+            recv_sem=z_recv.at[piece, k - 1],
+            device_id={"fn": lax.rem(me + 4 * k, n)},
+            device_id_type=MESH,
+        )
+
+    def last_copy(piece):
+        slot = Z_FIRST.index(piece)
+        return pltpu.make_async_remote_copy(
+            src_ref=last_send.at[slot],
+            dst_ref=from_last.at[slot],
+            send_sem=y_send.at[piece],
+            recv_sem=y_recv.at[piece],
+            device_id={"fn": other_y},
+            device_id_type=MESH,
+        )
+
+    def core_sum(piece, y, z):
+        return wide[piece, core * (n // 2) + y * nz + z] + from_core[piece, y * nz + z].astype(
+            f32
+        )
+
+    def core_to_lines(piece):
+        core_copy(piece).wait_recv()
+        for k in range(1, nz):
+            target = lax.rem(z_at + k, nz)
+            for y in range(2):
+                lines_send[Z_FIRST.index(piece), k - 1, y] = core_sum(piece, y, target).astype(
+                    bf16
+                )
+            line_copy(piece, k).start()
+
+    def lines_to_y(piece):
+        slot = Z_FIRST.index(piece)
+        away, own_sum = core_sum(piece, 1 - y_at, z_at), core_sum(piece, y_at, z_at)
+        for k in range(1, nz):
+            line_copy(piece, k).wait_recv()
+            away = away + from_lines[slot, k - 1, 1 - y_at].astype(f32)
+            own_sum = own_sum + from_lines[slot, k - 1, y_at].astype(f32)
+        last_send[slot] = away.astype(bf16)
+        last_copy(piece).start()
+        half_keep[piece, 0] = own_sum
+
     def core_to_y(piece):
+        if piece in Z_FIRST:
+            core_to_lines(piece)
+            return
         core_copy(piece).wait_recv()
         away = (1 - y_at) * nz
         half_send[piece] = (
@@ -400,6 +456,8 @@
         ].astype(f32)
 
     def y_to_z(piece):
+        if piece in Z_FIRST:
+            return
         y_copy(piece).wait_recv()
         for k in range(1, nz):
             target = lax.rem(z_at + k, nz)
@@ -409,6 +467,9 @@
             z_copy(piece, k).start()
 
     def finish(piece):
+        if piece in Z_FIRST:
+            last_copy(piece).wait_recv()
+            return half_keep[piece, 0] + from_last[Z_FIRST.index(piece)].astype(f32)
         total = half_keep[piece, z_at] + from_y[piece, z_at].astype(f32)
         for k in range(1, nz):
             z_copy(piece, k).wait_recv()
@@ -449,6 +510,8 @@
     for i in range(2 * unit, 4 * unit):
         core_to_y(i)
         y_to_z(i - 2 * unit + 1)
+    for piece in Z_FIRST:
+        lines_to_y(piece)
     for i in range(2 * unit + 1, 4 * unit):
         y_to_z(i)
     for i in range(4 * unit):
@@ -458,9 +521,9 @@
         points_copy(k).wait_send()
     for piece in range(4 * unit):
         core_copy(piece).wait_send()
-        y_copy(piece).wait_send()
+        (last_copy if piece in Z_FIRST else y_copy)(piece).wait_send()
         for k in range(1, nz):
-            z_copy(piece, k).wait_send()
+            (line_copy if piece in Z_FIRST else z_copy)(piece, k).wait_send()
 
 
 def far_first(n):
@@ -541,6 +604,10 @@
             pltpu.VMEM((pieces, n // 2, rows, width), bf16),
             pltpu.VMEM((pieces, nz, rows, width), bf16),
             pltpu.VMEM((pieces, nz - 1, rows, width), bf16),
+            pltpu.VMEM((len(Z_FIRST), nz - 1, 2, rows, width), bf16),
+            pltpu.VMEM((len(Z_FIRST), nz - 1, 2, rows, width), bf16),
+            pltpu.VMEM((len(Z_FIRST), rows, width), bf16),
+            pltpu.VMEM((len(Z_FIRST), rows, width), bf16),
             pltpu.SemaphoreType.DMA((len(operands),)),
             pltpu.SemaphoreType.DMA((n - 1,)),
             pltpu.SemaphoreType.DMA((n - 1,)),

time: 34.2 us -> 32.5 us (0.950)
  Pallas kernels: 33.4 us -> 31.7 us
    pallas_call x1, Pallas kernels: 31.7 us -> 30 us  [fused_step(): pl.pallas_call(functools.partial(step_kernel, n), out_shape=jax.ShapeDtyp...]
where the time goes in v3:
time: 32.5 us; the launch traced here: 32.3 us
  Pallas kernels  31.7 us (98%)
  between operations  0.64 us (2%)
    pallas_call x1, Pallas kernels, fused_step(): pl.pallas_call(functools.partial(step_kernel, n), out_shape=jax.ShapeDtyp...  30 us
    pallas_call x1, Pallas kernels, fused_step(): pl.pallas_call(split_kernel, out_shape=(jax.ShapeDtypeStruct((2 * out_row...  1.67 us

profile of v3, /device:TPU:0, one launch (start us, length us, event | category | flops | bytes accessed | tf_op | source)
XLA Modules:
  0.0 32.3 jit_solution(8588006850989751183)
XLA Ops:
  0.6 30.0 %shard_map.148.sums = f32[128,512]{1,0:T(8,128)} custom-call(bf16[256,1024]{1,0:T(8,128)(2,1)} %refs_0_.1, f32[1,256]{1,0:T(1,128)} %bitcast.13, s32[2,256]{1,0:T(2,128)} %bitcast.8, s32[2,8]{1,0:T(2,128)} %bitcast.14, bf16[1,8]{1,0:T(2,128)(2,1)} %bitcast.15, bf16[1024,512]{1,0:T(8,128)(2,1)} %refs_5_.1, f32[1,512]{1,0:T(1,128)} %bitcast.9, ...), custom_call_target="tpu_custom_call" | custom-call | tf_op jit(solution)/shard_map/pallas_call | solution.py:589
  30.6 1.7 %shard_map.149 = (f32[64,512]{1,0:T(8,128)}, f32[32,512]{1,0:T(8,128)}, f32[32,512]{1,0:T(8,128)}) custom-call(f32[128,512]{1,0:T(8,128)} %shard_map.148.sums), custom_call_target="tpu_custom_call" | custom-call | tf_op jit(solution)/shard_map/pallas_call | solution.py:625
